TPU v7x, 512 devices: a whole 4x8x8 slice. The times are simulated.
512 devices in a mesh: layer: 16 (over y, core), grid: 32 (over x, z).
Axes of the slice: x: 4, y: 8, z: 8, core: 2. Of those that a mesh axis runs over, the one named last changes fastest.
Arguments:
- l_panels: bfloat16 [16, 2, 8192, 512], P('layer', None, 'grid'), may hold values from -6 to 6
- u_panels: bfloat16 [16, 2, 512, 2048], P('layer', None, 'grid'), may hold values from -0.046875 to 0.046875
- panel_fill: int32 [16, 2, 64, 4], P('layer', None, 'grid'), may hold values 0 or 1
- copy_fill: int32 [16, 64, 16], P('layer', 'grid'), may hold values 0 or 1
- sep_panels: bfloat16 [15, 8192, 256], P(None, 'grid'), may hold values from -0.25 to 0.25
- sep_owner: int32 [15], replicated, may hold values from 0 to 31
Outputs:
- schur: float32 [8192, 2048], P('grid', 'layer')
All inputs are finite; a program needn't handle non-finite values. No bound on the sum of `panel_fill` or of `copy_fill` on one device may be relied on, other than what follows from the above.
Results may differ from a plain program's by a relative error of at most 0.0035.
Values may be sent and summed in bfloat16 or wider, within the bound.
A program may use at most 64 MiB of HBM per device.

v0:
```python
import jax
import jax.numpy as jnp
from jax import lax
from jax.sharding import PartitionSpec as P

BLOCK = 128


def from_partner(x, axis, apart):
    return lax.ppermute(x, axis, [(i, i ^ 1 << apart) for i in range(lax.axis_size(axis))])


def spread(x, axis, root):
    mine = lax.axis_index(axis) == root
    return lax.psum(jnp.where(mine, x, jnp.zeros_like(x)), axis)


def local(l_panels, u_panels, panel_fill, copy_fill, sep_panels, sep_owner):
    panel_count = l_panels.shape[1]
    row_count = l_panels.shape[2]
    panel_width = l_panels.shape[3]
    columns = u_panels.shape[3]
    fill_panel = panel_fill[0].astype(jnp.bfloat16)
    masked = (
        l_panels[0].reshape(panel_count, row_count // BLOCK, BLOCK, panel_width // BLOCK, BLOCK)
        * fill_panel[:, :, None, :, None]
    ).reshape(panel_count, row_count, panel_width)
    running = jnp.zeros((row_count, columns), jnp.float32)
    piece = lax.all_gather(u_panels, "grid", axis=2, tiled=True)
    for k in range(panel_count):
        column_part = masked[k]
        running = running + jnp.dot(column_part, piece[0, k], preferred_element_type=jnp.float32)
    fill_copy = copy_fill[0].astype(jnp.float32)
    layer_copy = -(
        running.reshape(row_count // BLOCK, BLOCK, columns // BLOCK, BLOCK)
        * fill_copy[:, None, :, None]
    ).reshape(row_count, columns)
    layers = lax.axis_size("layer")
    level_count = layers.bit_length() - 1
    layer_index = lax.axis_index("layer")
    column_width = columns // layers
    combined = layer_copy
    for level_index in range(level_count):
        partner = from_partner(combined, "layer", level_index)
        combined = combined + partner
        node_index = layers - (layers >> level_index) + (layer_index >> level_index + 1)
        owner_index = sep_owner[node_index]
        pivot_rows = spread(combined.astype(jnp.bfloat16), "grid", owner_index)
        factor = lax.dynamic_index_in_dim(sep_panels, node_index, 0, keepdims=False)
        combined = combined - jnp.dot(factor, pivot_rows, preferred_element_type=jnp.float32)
    return lax.dynamic_slice_in_dim(combined, layer_index * column_width, column_width, 1)


def solution(mesh):
    return jax.shard_map(
        local,
        mesh=mesh,
        in_specs=(
            P("layer", None, "grid", None),
            P("layer", None, "grid", None),
            P("layer", None, "grid", None),
            P("layer", "grid", None),
            P(None, "grid", None),
            P(),
        ),
        out_specs=P("grid", "layer"),
        check_vma=False,
    )
```

profile of v0, /device:TPU:8, one launch (start us, length us, event | category | flops | bytes accessed | tf_op | source)
XLA Modules:
  0.0 1016.5 jit_solution(16947582631460522231)
XLA Ops:
  6.5 0.7 all-gather.2.cloned.1.call-update
  7.3 1.2 reshape_squeeze.3
  8.5 0.7 convert_bitcast_fusion
  9.2 0.7 convert_bitcast_fusion.1
  9.8 0.3 broadcast_multiply_fusion
  10.2 0.2 fusion.20
  10.3 93.3 %all-gather.2.cloned.1.call-done = bf16[1,2,512,2048]{3,2,1,0:T(8,128)(2,1)} async-done(((bf16[1,2,16,2048]{3,2,1,0:T(8,128)(2,1)}), bf16[1,2,512,2048]{3,2,1,0:T(8,128)(2,1)}) %all-gather.2.cloned.1.call-update) | async-done | bytes 4194320 | tf_op jit(solution)/shard_map/all_gather | solution.py:29
  103.6 2.4 fusion.2
  106.1 0.2 mul.24
  106.4 2.5 fusion.1
  109.0 1.9 collective-permute-start
  110.9 0.7 fusion.21
  112.2 3.1 collective-permute-done
  115.4 4.4 convert_select_fusion.3
  119.9 157.3 %all-reduce.5.cloned.1.call-done = bf16[256,2048]{1,0:T(8,128)(2,1)} async-done(((bf16[256,2048]{1,0:T(8,128)(2,1)}), bf16[256,2048]{1,0:T(8,128)(2,1)}) %all-reduce.5.cloned.1.call-update) | async-done | bytes 1048592 | tf_op jit(solution)/shard_map/psum | solution.py:15
  277.2 3.7 convolution_subtract_fusion.2
  280.9 2.4 collective-permute-start.1
  283.9 41.9 %collective-permute-done.1 = f32[256,2048]{1,0:T(8,128)} collective-permute-done((f32[256,2048]{1,0:T(8,128)}, f32[256,2048]{1,0:T(8,128)}, u32[]{:S(2)}, u32[]{:S(2)}) %collective-permute-start.1) | collective-permute-done | bytes 2097184 | tf_op jit(solution)/shard_map/ppermute | solution.py:10
  325.9 4.4 convert_select_fusion.2
  330.4 158.1 %all-reduce.7.cloned.1.call-done = bf16[256,2048]{1,0:T(8,128)(2,1)} async-done(((bf16[256,2048]{1,0:T(8,128)(2,1)}), bf16[256,2048]{1,0:T(8,128)(2,1)}) %all-reduce.7.cloned.1.call-update) | async-done | bytes 1048592 | tf_op jit(solution)/shard_map/psum | solution.py:15
  488.5 3.7 convolution_subtract_fusion.1
  492.2 4.3 collective-permute-start.2
  497.1 85.0 %collective-permute-done.2 = f32[256,2048]{1,0:T(8,128)} collective-permute-done((f32[256,2048]{1,0:T(8,128)}, f32[256,2048]{1,0:T(8,128)}, u32[]{:S(2)}, u32[]{:S(2)}) %collective-permute-start.2) | collective-permute-done | bytes 2097184 | tf_op jit(solution)/shard_map/ppermute | solution.py:10
  582.0 4.4 convert_select_fusion.1
  586.5 159.1 %all-reduce.9.cloned.1.call-done = bf16[256,2048]{1,0:T(8,128)(2,1)} async-done(((bf16[256,2048]{1,0:T(8,128)(2,1)}), bf16[256,2048]{1,0:T(8,128)(2,1)}) %all-reduce.9.cloned.1.call-update) | async-done | bytes 1048592 | tf_op jit(solution)/shard_map/psum | solution.py:15
  745.7 3.7 convolution_subtract_fusion
  749.4 6.5 collective-permute-start.3
  756.4 87.0 %collective-permute-done.3 = f32[256,2048]{1,0:T(8,128)} collective-permute-done((f32[256,2048]{1,0:T(8,128)}, f32[256,2048]{1,0:T(8,128)}, u32[]{:S(2)}, u32[]{:S(2)}) %collective-permute-start.3) | collective-permute-done | bytes 2097184 | tf_op jit(solution)/shard_map/ppermute | solution.py:10
  843.5 4.4 convert_select_fusion
  847.9 158.8 %all-reduce.11.cloned.1.call-done = bf16[256,2048]{1,0:T(8,128)(2,1)} async-done(((bf16[256,2048]{1,0:T(8,128)(2,1)}), bf16[256,2048]{1,0:T(8,128)(2,1)}) %all-reduce.11.cloned.1.call-update) | async-done | bytes 1048592 | tf_op jit(solution)/shard_map/psum | solution.py:15
  1006.7 1.7 fusion.7
  1008.4 1.6 dynamic-slice_subtract_fusion
  (15 shorter events, 0.4 us)
Async XLA Ops:
  6.5 270.6 %copy-start = (bf16[15,256,256]{2,1,0:T(8,128)(2,1)S(1)}, bf16[15,256,256]{2,1,0:T(8,128)(2,1)}, u32[]{:S(2)}) copy-start(bf16[15,256,256]{2,1,0:T(8,128)(2,1)} %param.10) | copy-start | bytes 5898244
  6.5 97.1 %all-gather.2.cloned.1.call-start = ((), (), s32[]{:S(2)}) async-start(), calls=%async_computation | async-start | bytes 4325376 | tf_op jit(solution)/shard_map/all_gather | solution.py:29
  7.3 269.9 %all-reduce.5.cloned.1.call-start = ((), (), s32[]{:S(2)}) async-start(), calls=%async_computation.1 | async-start | bytes 2097152 | tf_op jit(solution)/shard_map/psum | solution.py:15
  103.6 2.8 copy-start.1
  106.4 4.5 copy-start.2
  109.0 6.4 collective-permute-start
  119.8 368.7 %all-reduce.7.cloned.1.call-start = ((), (), s32[]{:S(2)}) async-start(), calls=%async_computation.2 | async-start | bytes 2097152 | tf_op jit(solution)/shard_map/psum | solution.py:15
  280.9 45.0 %collective-permute-start.1 = (f32[256,2048]{1,0:T(8,128)}, f32[256,2048]{1,0:T(8,128)}, u32[]{:S(2)}, u32[]{:S(2)}) collective-permute-start(f32[256,2048]{1,0:T(8,128)} %convolution_subtract_fusion.2), channel_id=1, source_target_pairs={{0,64},{32,96},{64,0},{96,32},{128,192},{160,224},{192,128},{224,1... | collective-permute-start | bytes 6291464 | tf_op jit(solution)/shard_map/ppermute | solution.py:10
  330.3 415.3 %all-reduce.9.cloned.1.call-start = ((), (), s32[]{:S(2)}) async-start(), calls=%async_computation.3 | async-start | bytes 2097152 | tf_op jit(solution)/shard_map/psum | solution.py:15
  492.2 89.9 %collective-permute-start.2 = (f32[256,2048]{1,0:T(8,128)}, f32[256,2048]{1,0:T(8,128)}, u32[]{:S(2)}, u32[]{:S(2)}) collective-permute-start(f32[256,2048]{1,0:T(8,128)} %convolution_subtract_fusion.1), channel_id=1, source_target_pairs={{0,128},{32,160},{64,192},{96,224},{128,0},{160,32},{192,64},{224,... | collective-permute-start | bytes 6291464 | tf_op jit(solution)/shard_map/ppermute | solution.py:10
  586.5 420.2 %all-reduce.11.cloned.1.call-start = ((), (), s32[]{:S(2)}) async-start(), calls=%async_computation.4 | async-start | bytes 2097152 | tf_op jit(solution)/shard_map/psum | solution.py:15
  749.4 94.1 %collective-permute-start.3 = (f32[256,2048]{1,0:T(8,128)}, f32[256,2048]{1,0:T(8,128)}, u32[]{:S(2)}, u32[]{:S(2)}) collective-permute-start(f32[256,2048]{1,0:T(8,128)} %convolution_subtract_fusion), channel_id=1, source_target_pairs={{0,256},{32,288},{64,320},{96,352},{128,384},{160,416},{192,448},{... | collective-permute-start | bytes 6291464 | tf_op jit(solution)/shard_map/ppermute | solution.py:10
Sparse Core Ops, SparseCore 0:
  10.5 93.0 all-gather.1
  119.9 157.1 all-reduce.4
  330.5 157.9 all-reduce.6
  586.6 159.0 all-reduce.8
  848.0 158.6 all-reduce.10
where the time goes:
time: 1020 us
  waiting for transfers between devices  944 us (93%)
  other arithmetic  21 us (2%)
  matrix products  17.7 us (2%)
  between operations  15.7 us (2%)
  starting transfers between devices  15.3 us (2%)
    psum x4, waiting for transfers between devices, spread(): return lax.psum(jnp.where(mine, x, jnp.zeros_like(x)), axis)  633 us
    ppermute x4, waiting for transfers between devices, from_partner(): lax.ppermute(x, axis, [(i, i ^ 1 << apart) for i in range(lax.axis_size(a...  217 us
    all_gather x1, waiting for transfers between devices, local(): piece = lax.all_gather(u_panels, 'grid', axis=2, tiled=True)  93.3 us
  transfers between devices with their start and end apart: 9, of which 9 were waited for; matrix products, arithmetic and copies ran while one was open for 0% of the time, Pallas kernels for 0%

commit v1 on v0

--- a/solution.py
+++ b/solution.py
@@ -6,13 +6,19 @@
 BLOCK = 128
 
 
+def summed_here(x, axis):
+    terms = lax.all_gather(x, axis, axis=0, tiled=False)
+    total = terms.sum(axis=0)
+    return total
+
+
 def from_partner(x, axis, apart):
     return lax.ppermute(x, axis, [(i, i ^ 1 << apart) for i in range(lax.axis_size(axis))])
 
 
 def spread(x, axis, root):
     mine = lax.axis_index(axis) == root
-    return lax.psum(jnp.where(mine, x, jnp.zeros_like(x)), axis)
+    return summed_here(jnp.where(mine, x, jnp.zeros_like(x)), axis)
 
 
 def local(l_panels, u_panels, panel_fill, copy_fill, sep_panels, sep_owner):

time: 1020 us -> 1390 us (1.36)
  the two profiles are of different devices: /device:TPU:8 before, /device:TPU:1 now
where the time goes in v1:
time: 1390 us
  waiting for transfers between devices  1270 us (91%)
  other arithmetic  66.6 us (5%)
  starting transfers between devices  20.4 us (1%)
  between operations  15.7 us (1%)
  matrix products  15.6 us (1%)
    all_gather x4, waiting for transfers between devices, summed_here(): terms = lax.all_gather(x, axis, axis=0, tiled=False)  956 us
    ppermute x4, waiting for transfers between devices, from_partner(): lax.ppermute(x, axis, [(i, i ^ 1 << apart) for i in range(lax.axis_size(a...  218 us
    all_gather x1, waiting for transfers between devices, local(): piece = lax.all_gather(u_panels, 'grid', axis=2, tiled=True)  90.8 us
    reduce_sum x4, other arithmetic, summed_here(): total = terms.sum(axis=0)  45.8 us
  transfers between devices with their start and end apart: 9, of which 9 were waited for; matrix products, arithmetic and copies ran while one was open for 0% of the time, Pallas kernels for 0%

profile of v1, /device:TPU:1, one launch (start us, length us, event | category | flops | bytes accessed | tf_op | source)
XLA Modules:
  0.0 1386.0 jit_solution(14904285957876874924)
XLA Ops:
  6.5 0.7 all-gather.10.cloned.1.call-update
  7.3 1.2 reshape_squeeze.3
  8.5 0.7 convert_bitcast_fusion
  9.2 0.7 convert_bitcast_fusion.1
  10.3 90.8 %all-gather.10.cloned.1.call-done = bf16[1,2,512,2048]{3,2,1,0:T(8,128)(2,1)} async-done(((bf16[1,2,16,2048]{3,2,1,0:T(8,128)(2,1)}), bf16[1,2,512,2048]{3,2,1,0:T(8,128)(2,1)}) %all-gather.10.cloned.1.call-update) | async-done | bytes 4194320 | tf_op jit(solution)/shard_map/all_gather | solution.py:35
  101.1 2.4 fusion.2
  103.9 2.5 fusion.1
  106.5 6.0 collective-permute-start
  112.5 0.6 fusion.21
  113.8 2.8 collective-permute-done
  116.6 4.4 convert_select_fusion.3
  121.0 235.3 %all-gather.12.cloned.1.call-done = bf16[8192,2048]{1,0:T(8,128)(2,1)} async-done(((bf16[256,2048]{1,0:T(8,128)(2,1)}), bf16[8192,2048]{1,0:T(8,128)(2,1)}) %all-gather.12.cloned.1.call-update) | async-done | bytes 33554448 | tf_op jit(solution)/shard_map/all_gather | solution.py:10
  356.3 11.5 reduce_sum.48
  367.7 3.4 convolution_subtract_fusion.2
  371.2 3.1 collective-permute-start.1
  374.9 44.6 %collective-permute-done.1 = f32[256,2048]{1,0:T(8,128)} collective-permute-done((f32[256,2048]{1,0:T(8,128)}, f32[256,2048]{1,0:T(8,128)}, u32[]{:S(2)}, u32[]{:S(2)}) %collective-permute-start.1) | collective-permute-done | bytes 2097184 | tf_op jit(solution)/shard_map/ppermute | solution.py:16
  419.4 4.4 convert_select_fusion.2
  423.9 237.1 %all-gather.14.cloned.1.call-done = bf16[8192,2048]{1,0:T(8,128)(2,1)} async-done(((bf16[256,2048]{1,0:T(8,128)(2,1)}), bf16[8192,2048]{1,0:T(8,128)(2,1)}) %all-gather.14.cloned.1.call-update) | async-done | bytes 33554448 | tf_op jit(solution)/shard_map/all_gather | solution.py:10
  661.0 11.5 reduce_sum.49
  672.5 3.4 convolution_subtract_fusion.1
  675.8 4.0 collective-permute-start.2
  680.4 90.0 %collective-permute-done.2 = f32[256,2048]{1,0:T(8,128)} collective-permute-done((f32[256,2048]{1,0:T(8,128)}, f32[256,2048]{1,0:T(8,128)}, u32[]{:S(2)}, u32[]{:S(2)}) %collective-permute-start.2) | collective-permute-done | bytes 2097184 | tf_op jit(solution)/shard_map/ppermute | solution.py:16
  770.5 4.4 convert_select_fusion.1
  774.9 236.7 %all-gather.16.cloned.1.call-done = bf16[8192,2048]{1,0:T(8,128)(2,1)} async-done(((bf16[256,2048]{1,0:T(8,128)(2,1)}), bf16[8192,2048]{1,0:T(8,128)(2,1)}) %all-gather.16.cloned.1.call-update) | async-done | bytes 33554448 | tf_op jit(solution)/shard_map/all_gather | solution.py:10
  1011.5 11.5 reduce_sum.50
  1023.0 3.4 convolution_subtract_fusion
  1026.4 7.1 collective-permute-start.3
  1034.1 80.9 %collective-permute-done.3 = f32[256,2048]{1,0:T(8,128)} collective-permute-done((f32[256,2048]{1,0:T(8,128)}, f32[256,2048]{1,0:T(8,128)}, u32[]{:S(2)}, u32[]{:S(2)}) %collective-permute-start.3) | collective-permute-done | bytes 2097184 | tf_op jit(solution)/shard_map/ppermute | solution.py:16
  1115.0 4.4 convert_select_fusion
  1119.5 246.5 %all-gather.18.cloned.1.call-done = bf16[8192,2048]{1,0:T(8,128)(2,1)} async-done(((bf16[256,2048]{1,0:T(8,128)(2,1)}), bf16[8192,2048]{1,0:T(8,128)(2,1)}) %all-gather.18.cloned.1.call-update) | async-done | bytes 33554448 | tf_op jit(solution)/shard_map/all_gather | solution.py:10
  1366.0 11.5 reduce_sum.51
  1377.9 1.6 dynamic-slice_subtract_fusion
  (19 shorter events, 1.5 us)
Async XLA Ops:
  6.5 361.2 %copy-start = (bf16[15,256,256]{2,1,0:T(8,128)(2,1)S(1)}, bf16[15,256,256]{2,1,0:T(8,128)(2,1)}, u32[]{:S(2)}) copy-start(bf16[15,256,256]{2,1,0:T(8,128)(2,1)} %param.10) | copy-start | bytes 5898244
  6.5 94.6 %all-gather.10.cloned.1.call-start = ((), (), s32[]{:S(2)}) async-start(), calls=%async_computation | async-start | bytes 4325376 | tf_op jit(solution)/shard_map/all_gather | solution.py:35
  7.3 349.0 %all-gather.12.cloned.1.call-start = ((), (), s32[]{:S(2)}) async-start(), calls=%async_computation.1 | async-start | bytes 34603008 | tf_op jit(solution)/shard_map/all_gather | solution.py:10
  101.1 2.8 copy-start.1
  103.9 8.6 copy-start.2
  106.5 10.1 collective-permute-start
  121.0 540.1 %all-gather.14.cloned.1.call-start = ((), (), s32[]{:S(2)}) async-start(), calls=%async_computation.2 | async-start | bytes 34603008 | tf_op jit(solution)/shard_map/all_gather | solution.py:10
  371.2 48.3 %collective-permute-start.1 = (f32[256,2048]{1,0:T(8,128)}, f32[256,2048]{1,0:T(8,128)}, u32[]{:S(2)}, u32[]{:S(2)}) collective-permute-start(f32[256,2048]{1,0:T(8,128)} %convolution_subtract_fusion.2), channel_id=1, source_target_pairs={{0,64},{32,96},{64,0},{96,32},{128,192},{160,224},{192,128},{224,1... | collective-permute-start | bytes 6291464 | tf_op jit(solution)/shard_map/ppermute | solution.py:16
  423.9 587.7 %all-gather.16.cloned.1.call-start = ((), (), s32[]{:S(2)}) async-start(), calls=%async_computation.3 | async-start | bytes 34603008 | tf_op jit(solution)/shard_map/all_gather | solution.py:10
  675.8 94.6 %collective-permute-start.2 = (f32[256,2048]{1,0:T(8,128)}, f32[256,2048]{1,0:T(8,128)}, u32[]{:S(2)}, u32[]{:S(2)}) collective-permute-start(f32[256,2048]{1,0:T(8,128)} %convolution_subtract_fusion.1), channel_id=1, source_target_pairs={{0,128},{32,160},{64,192},{96,224},{128,0},{160,32},{192,64},{224,... | collective-permute-start | bytes 6291464 | tf_op jit(solution)/shard_map/ppermute | solution.py:16
  774.8 591.2 %all-gather.18.cloned.1.call-start = ((), (), s32[]{:S(2)}) async-start(), calls=%async_computation.4 | async-start | bytes 34603008 | tf_op jit(solution)/shard_map/all_gather | solution.py:10
  1026.4 88.6 %collective-permute-start.3 = (f32[256,2048]{1,0:T(8,128)}, f32[256,2048]{1,0:T(8,128)}, u32[]{:S(2)}, u32[]{:S(2)}) collective-permute-start(f32[256,2048]{1,0:T(8,128)} %convolution_subtract_fusion), channel_id=1, source_target_pairs={{0,256},{32,288},{64,320},{96,352},{128,384},{160,416},{192,448},{... | collective-permute-start | bytes 6291464 | tf_op jit(solution)/shard_map/ppermute | solution.py:16
Sparse Core Ops, SparseCore 0:
  10.5 90.5 all-gather.9
  121.1 235.1 all-gather.11
  424.0 237.0 all-gather.13
  775.0 236.5 all-gather.15
  1119.6 246.3 all-gather.17
